TPU v7x, 768 devices: a whole 4x8x12 slice. The times are simulated.
768 devices in a mesh: sx: 48 (over y, z_lo), sy: 16 (over z_hi, x, core).
Axes of the slice: x: 4, y: 8, z: 12 (z_hi: 2, z_lo: 6; z = z_hi * 6 + z_lo), core: 2. Of those that a mesh axis runs over, the one named last changes fastest.
Arguments:
- schur: bfloat16 [48, 4096, 4096], P('sx', 'sy'), as said below
- precond: bfloat16 [48, 4096, 4096], P('sx', 'sy'), as said below
- right_side: float32 [48, 32, 2048], P('sx', None, 'sy')
- matching: int32 [48, 2048], P('sx', 'sy'), may hold values from 0 to 127, as said below
Outputs:
- solution: float32 [48, 32, 2048], P('sx', None, 'sy')
- residual: float32 [48, 32, 2048], P('sx', None, 'sy')
Inputs may be any that keep to these rules, and one draw needn't show every extreme that they name: `schur`: each subdomain's matrix is symmetric positive definite. `precond`: each subdomain's matrix is symmetric positive definite. `matching`: each aligned block of 128 entries of a row is a permutation of 0 to 127.
All inputs are finite; a program needn't handle non-finite values.
Results may differ from a plain program's by a relative error of at most 0.007.
The roundings to bfloat16 on the way count: a program that leaves them out, or rounds other values in their place, can miss the bound.
Values may be sent and summed in bfloat16 or wider, within the bound.
A program may use at most 32 MiB of HBM per device.

v0:
```python
import jax
import jax.numpy as jnp
from jax import lax
from jax.sharding import PartitionSpec as P

ITERS = 2


def passed_along(block, axis, distance):
    devices = range(lax.axis_size(axis))
    route = [((i - distance) % len(devices), i) for i in devices]
    return lax.ppermute(block, axis, route)


def apply_op(matrix, block, match_loc, inverse):
    rows_here = matrix.shape[0]
    half = rows_here // 2
    sent = jnp.take(block, match_loc, axis=1)
    right_part = passed_along(sent, "sx", -1)
    local = jnp.concatenate([block, right_part], axis=1)
    prod = lax.dot_general(
        lax.all_gather(local, "sy", axis=1, tiled=True),
        matrix,
        (((1,), (1,)), ((), ())),
        preferred_element_type=jnp.float32,
    )
    left_out = prod[:, :half]
    right_out = prod[:, half:]
    came = passed_along(right_out, "sx", 1)
    return left_out + jnp.take(came, inverse, axis=1)


def gram(first, second):
    partial_sum = jnp.dot(first, second.T, precision=lax.Precision.HIGHEST)
    total = lax.psum(partial_sum, ("sx", "sy"))
    return 0.5 * (total + total.T)


def solve_spd(matrix, rhs):
    lower = jnp.linalg.cholesky(matrix)
    return jax.scipy.linalg.cho_solve((lower, True), rhs)


def combine(coeff, block):
    return jnp.dot(coeff.T, block, precision=lax.Precision.HIGHEST)


def shards(schur, precond, right_side, matching):
    schur_rows = schur[0]
    precond_rows = precond[0]
    match_loc = matching[0]
    inverse = jnp.argsort(match_loc)
    residual = right_side[0]
    solution = jnp.zeros_like(residual)
    search = apply_op(precond_rows, residual.astype(jnp.bfloat16), match_loc, inverse)
    gamma = gram(residual, search)
    for step in range(ITERS):
        image = apply_op(schur_rows, search.astype(jnp.bfloat16), match_loc, inverse)
        delta = gram(search, image)
        alpha = solve_spd(delta, gamma)
        solution = solution + combine(alpha, search)
        residual = residual - combine(alpha, image)
        if step + 1 < ITERS:
            precd = apply_op(precond_rows, residual.astype(jnp.bfloat16), match_loc, inverse)
            gnew = gram(residual, precd)
            beta = solve_spd(gamma, gnew)
            search = precd + combine(beta, search)
            gamma = gnew
    return (solution[None], residual[None])


def solution(mesh):
    in_specs = (P("sx", "sy", None), P("sx", "sy", None), P("sx", None, "sy"), P("sx", "sy"))
    out_specs = (P("sx", None, "sy"), P("sx", None, "sy"))
    return jax.shard_map(shards, mesh=mesh, in_specs=in_specs, out_specs=out_specs, check_vma=False)
```

profile of v0, /device:TPU:1, one launch (start us, length us, event | category | flops | bytes accessed | tf_op | source)
XLA Modules:
  0.0 574.3 jit_solution(17957201035716055342)
XLA Ops:
  0.6 0.8 compare_and_fusion.1
  1.5 0.7 compare_select_fusion.1
  2.1 0.7 bitcast_convert_fusion
  3.0 0.7 gather_fusion
  3.8 16.2 %collective-permute-start = (bf16[32,128]{1,0:T(8,128)(2,1)S(1)}, bf16[32,128]{1,0:T(8,128)(2,1)S(1)}, u32[]{:S(2)}, u32[]{:S(2)}) collective-permute-start(bf16[32,128]{1,0:T(8,128)(2,1)S(1)} %select_bitcast_fusion.3), channel_id=1, source_target_pairs={{16,0},{32,16},{48,32},{64,48},{80,64},{96,80},{112,96},{128,112},... | collective-permute-start | bytes 24584 | tf_op jit(solution)/shard_map/ppermute | solution.py:12
  20.0 3.2 sort.17
  23.2 40.4 %all_gather.12 = bf16[32,4096]{1,0:T(8,128)(2,1)S(1)} all-gather(bf16[32,256]{1,0:T(8,128)(2,1)S(1)} %pad_maximum_fusion), channel_id=1, replica_groups=mesh['sx'=48,'sy'=16] {'sy'}, dimensions={1}, use_global_device_ids=true | all-gather | bytes 278528 | tf_op jit(solution)/shard_map/all_gather | solution.py:22
  63.6 0.7 fusion.6
  64.3 1.9 collective-permute-start.1
  66.3 9.5 %collective-permute-done.1 = f32[32,128]{1,0:T(8,128)S(1)} collective-permute-done((f32[32,128]{1,0:T(8,128)S(1)}, f32[32,128]{1,0:T(8,128)S(1)}, u32[]{:S(2)}, u32[]{:S(2)}) %collective-permute-start.1) | collective-permute-done | bytes 16416 | tf_op jit(solution)/shard_map/ppermute | solution.py:12
  75.8 0.6 gather_fusion.1
  76.7 0.7 gather_fusion.2
  77.5 1.9 collective-permute-start.2
  79.4 2.5 collective-permute-done.2
  81.9 31.6 %all_gather.13 = bf16[32,4096]{1,0:T(8,128)(2,1)S(1)} all-gather(bf16[32,256]{1,0:T(8,128)(2,1)S(1)} %pad_maximum_fusion.1), channel_id=1, replica_groups=mesh['sx'=48,'sy'=16] {'sy'}, dimensions={1}, use_global_device_ids=true | all-gather | bytes 278528 | tf_op jit(solution)/shard_map/all_gather | solution.py:22
  113.5 2.3 fusion.2
  115.8 1.9 collective-permute-start.3
  117.9 9.3 %collective-permute-done.3 = f32[32,128]{1,0:T(8,128)S(1)} collective-permute-done((f32[32,128]{1,0:T(8,128)S(1)}, f32[32,128]{1,0:T(8,128)S(1)}, u32[]{:S(2)}, u32[]{:S(2)}) %collective-permute-start.3) | collective-permute-done | bytes 16416 | tf_op jit(solution)/shard_map/ppermute | solution.py:12
  127.3 0.6 gather_fusion.3
  128.0 0.2 fusion.35
  128.2 105.1 %all-reduce = (f32[32,32]{1,0:T(8,128)S(1)}, f32[32,32]{1,0:T(8,128)S(1)}) all-reduce(f32[32,32]{1,0:T(8,128)S(1)} %convolution_bitcast_fusion, f32[32,32]{1,0:T(8,128)S(1)} %fusion.35), channel_id=1, replica_groups=mesh['sx'=48,'sy'=16] {'sx','sy'}, use_global_device_ids=true, to_apply=%region_4.8 | all-reduce | flops 2048 | bytes 16384 | tf_op jit(solution)/shard_map/psum | solution.py:35
  233.6 2.9 cholesky.59
  236.5 0.6 compare_reduce_fusion.2
  237.2 0.7 fusion.10
  237.8 2.4 custom-call.9
  240.3 0.2 fusion.28
  240.5 0.1 fusion.26
  240.7 0.2 fusion.46
  241.0 2.9 cholesky.70
  244.0 0.7 gather_fusion.4
  244.8 3.7 collective-permute-start.4
  248.6 0.6 compare_reduce_fusion.1
  249.2 0.3 collective-permute-done.4
  249.5 36.1 %all_gather.14 = bf16[32,4096]{1,0:T(8,128)(2,1)S(1)} all-gather(bf16[32,256]{1,0:T(8,128)(2,1)S(1)} %pad_maximum_fusion.2), channel_id=1, replica_groups=mesh['sx'=48,'sy'=16] {'sy'}, dimensions={1}, use_global_device_ids=true | all-gather | bytes 278528 | tf_op jit(solution)/shard_map/all_gather | solution.py:22
  285.7 0.7 fusion.4
  286.4 1.9 collective-permute-start.5
  288.3 0.7 fusion.11
  289.0 2.4 custom-call.10
  291.4 6.4 %collective-permute-done.5 = f32[32,128]{1,0:T(8,128)S(1)} collective-permute-done((f32[32,128]{1,0:T(8,128)S(1)}, f32[32,128]{1,0:T(8,128)S(1)}, u32[]{:S(2)}, u32[]{:S(2)}) %collective-permute-start.5) | collective-permute-done | bytes 16416 | tf_op jit(solution)/shard_map/ppermute | solution.py:12
  297.9 0.6 gather_fusion.5
  298.6 0.2 fusion.36
  298.8 104.3 %psum.30 = f32[32,32]{1,0:T(8,128)S(1)} all-reduce(f32[32,32]{1,0:T(8,128)S(1)} %fusion.36), channel_id=1, replica_groups=mesh['sx'=48,'sy'=16] {'sx','sy'}, use_global_device_ids=true, to_apply=%region_5.10 | all-reduce | flops 1024 | bytes 8192 | tf_op jit(solution)/shard_map/psum | solution.py:35
  403.2 0.2 fusion.22
  403.4 0.1 fusion.20
  403.6 0.2 fusion.47
  403.9 0.7 gather_fusion.6
  404.7 4.4 collective-permute-start.6
  409.2 0.8 collective-permute-done.6
  410.0 36.4 %all_gather.15 = bf16[32,4096]{1,0:T(8,128)(2,1)S(1)} all-gather(bf16[32,256]{1,0:T(8,128)(2,1)S(1)} %pad_maximum_fusion.3), channel_id=1, replica_groups=mesh['sx'=48,'sy'=16] {'sy'}, dimensions={1}, use_global_device_ids=true | all-gather | bytes 278528 | tf_op jit(solution)/shard_map/all_gather | solution.py:22
  446.4 2.3 fusion
  448.7 1.9 collective-permute-start.7
  450.6 0.2 fusion.48
  450.8 9.3 %collective-permute-done.7 = f32[32,128]{1,0:T(8,128)S(1)} collective-permute-done((f32[32,128]{1,0:T(8,128)S(1)}, f32[32,128]{1,0:T(8,128)S(1)}, u32[]{:S(2)}, u32[]{:S(2)}) %collective-permute-start.7) | collective-permute-done | bytes 16416 | tf_op jit(solution)/shard_map/ppermute | solution.py:12
  460.2 0.6 gather_fusion.7
  460.9 0.2 fusion.37
  461.1 104.3 %psum.31 = f32[32,32]{1,0:T(8,128)S(1)} all-reduce(f32[32,32]{1,0:T(8,128)S(1)} %fusion.37), channel_id=1, replica_groups=mesh['sx'=48,'sy'=16] {'sx','sy'}, use_global_device_ids=true, to_apply=%region_6.11 | all-reduce | flops 1024 | bytes 8192 | tf_op jit(solution)/shard_map/psum | solution.py:35
  565.6 2.9 cholesky.81
  568.5 0.6 compare_reduce_fusion
  569.2 0.7 fusion.12
  569.8 2.4 custom-call.11
  572.3 0.2 fusion.15
  572.5 0.1 fusion.13
  572.6 0.8 fusion.8
  573.5 0.8 fusion.9
  (55 shorter events, 2.3 us)
Async XLA Ops:
  0.6 62.9 %copy-start = (bf16[1,256,4096]{2,1,0:T(8,128)(2,1)S(1)}, bf16[1,256,4096]{2,1,0:T(8,128)(2,1)}, u32[]{:S(2)}) copy-start(bf16[1,256,4096]{2,1,0:T(8,128)(2,1)} %param.12) | copy-start | bytes 6291460
  3.8 19.4 %collective-permute-start = (bf16[32,128]{1,0:T(8,128)(2,1)S(1)}, bf16[32,128]{1,0:T(8,128)(2,1)S(1)}, u32[]{:S(2)}, u32[]{:S(2)}) collective-permute-start(bf16[32,128]{1,0:T(8,128)(2,1)S(1)} %select_bitcast_fusion.3), channel_id=1, source_target_pairs={{16,0},{32,16},{48,32},{64,48},{80,64},{96,80},{112,96},{128,112},... | collective-permute-start | bytes 24584 | tf_op jit(solution)/shard_map/ppermute | solution.py:12
  64.3 53.4 %copy-start.1 = (f32[1,32,128]{2,1,0:T(8,128)S(1)}, f32[1,32,128]{2,1,0:T(8,128)}, u32[]{:S(2)}) copy-start(f32[1,32,128]{2,1,0:T(8,128)} %param.13) | copy-start | bytes 49156
  64.3 11.4 %collective-permute-start.1 = (f32[32,128]{1,0:T(8,128)S(1)}, f32[32,128]{1,0:T(8,128)S(1)}, u32[]{:S(2)}, u32[]{:S(2)}) collective-permute-start(f32[32,128]{1,0:T(8,128)S(1)} %slice.61), channel_id=1, source_target_pairs={{752,0},{0,16},{16,32},{32,48},{48,64},{64,80},{80,96},{96,112},{1... | collective-permute-start | bytes 49160 | tf_op jit(solution)/shard_map/ppermute | solution.py:12
  77.5 4.4 collective-permute-start.2
  115.8 11.4 %collective-permute-start.3 = (f32[32,128]{1,0:T(8,128)S(1)}, f32[32,128]{1,0:T(8,128)S(1)}, u32[]{:S(2)}, u32[]{:S(2)}) collective-permute-start(f32[32,128]{1,0:T(8,128)S(1)} %slice.63), channel_id=1, source_target_pairs={{752,0},{0,16},{16,32},{32,48},{48,64},{64,80},{80,96},{96,112},{1... | collective-permute-start | bytes 49160 | tf_op jit(solution)/shard_map/ppermute | solution.py:12
  244.8 4.7 collective-permute-start.4
  286.4 11.4 %collective-permute-start.5 = (f32[32,128]{1,0:T(8,128)S(1)}, f32[32,128]{1,0:T(8,128)S(1)}, u32[]{:S(2)}, u32[]{:S(2)}) collective-permute-start(f32[32,128]{1,0:T(8,128)S(1)} %slice.65), channel_id=1, source_target_pairs={{752,0},{0,16},{16,32},{32,48},{48,64},{64,80},{80,96},{96,112},{1... | collective-permute-start | bytes 49160 | tf_op jit(solution)/shard_map/ppermute | solution.py:12
  404.7 5.2 collective-permute-start.6
  448.7 11.4 %collective-permute-start.7 = (f32[32,128]{1,0:T(8,128)S(1)}, f32[32,128]{1,0:T(8,128)S(1)}, u32[]{:S(2)}, u32[]{:S(2)}) collective-permute-start(f32[32,128]{1,0:T(8,128)S(1)} %slice.67), channel_id=1, source_target_pairs={{752,0},{0,16},{16,32},{32,48},{48,64},{64,80},{80,96},{96,112},{1... | collective-permute-start | bytes 49160 | tf_op jit(solution)/shard_map/ppermute | solution.py:12
where the time goes:
time: 575 us; the launch traced here: 574 us
  blocking collectives  458 us (80%)
  waiting for transfers between devices  38 us (7%)
  starting transfers between devices  33.9 us (6%)
  other arithmetic  25.6 us (4%)
  matrix products  10.1 us (2%)
  local copies, waits for them, and re-layouts  7.37 us (1%)
    psum x3, blocking collectives, gram(): total = lax.psum(partial_sum, ('sx', 'sy'))  314 us
    all_gather x4, blocking collectives, apply_op(): lax.all_gather(local, 'sy', axis=1, tiled=True)  144 us
    ppermute x8, waiting for transfers between devices, passed_along(): return lax.ppermute(block, axis, route)  38 us
    ppermute x8, starting transfers between devices, passed_along(): return lax.ppermute(block, axis, route)  33.9 us
  transfers between devices with their start and end apart: 8, of which 7 were waited for; matrix products, arithmetic and copies ran while one was open for 1% of the time, Pallas kernels for 0%

commit v1 on v0

v1 whole, which is shorter than its diff:
```python
import functools

import jax
import jax.numpy as jnp
from jax import lax
from jax.experimental import pallas as pl
from jax.experimental.pallas import tpu as pltpu
from jax.sharding import PartitionSpec as P

F32, BF16 = jnp.float32, jnp.bfloat16
MESH = pl.DeviceIdType.MESH
NY, NZL, NZH, NXC = 8, 6, 2, 8
NZ = NZL * NZH
K, FB = 32, 128


def split3(value):
    high = value.astype(BF16)
    rest = value - high.astype(F32)
    middle = rest.astype(BF16)
    low = (rest - middle.astype(F32)).astype(BF16)
    return high, middle, low


def moved(value, onehot, dim):
    parts = jnp.concatenate(split3(value), axis=0)
    out = lax.dot_general(parts, onehot, (((1,), (dim,)), ((), ())), preferred_element_type=F32)
    return out[:K] + out[K : 2 * K] + out[2 * K :]


def coeff_stack(coeff):
    a, b, c = split3(coeff)
    return jnp.concatenate([a, b, c, a, b, a], axis=0)


def value_stack(a, b, c):
    return jnp.concatenate([a, a, a, b, b, c], axis=0)


def combine(coeffs, values):
    return lax.dot_general(coeffs, values, (((0,), (0,)), ((), ())), preferred_element_type=F32)


def gram_part(first, second):
    one = jnp.concatenate(split3(jnp.concatenate([first, second], axis=1)), axis=0)
    two = jnp.concatenate(split3(jnp.concatenate([second, first], axis=1)), axis=0)
    out = lax.dot_general(one, two, (((1,), (1,)), ((), ())), preferred_element_type=F32)
    rows = out[:K] + out[K : 2 * K] + out[2 * K :]
    total = 0.5 * (rows[:, :K] + rows[:, K : 2 * K] + rows[:, 2 * K :])
    return jnp.concatenate([total[8 * a : 8 * a + 8] for a in range(4)], axis=1)


def unpacked(packed):
    return jnp.concatenate([packed[:, K * a : K * a + K] for a in range(4)], axis=0)


def solve(matrix, rhs):
    work = jnp.concatenate([matrix, rhs], axis=1)
    row_no = lax.broadcasted_iota(jnp.int32, work.shape, 0)
    for k in range(K):
        col = work[:, k : k + 1]
        row = work[k : k + 1, :]
        scaled = row * (1.0 / work[k : k + 1, k : k + 1])
        work = jnp.where(row_no == k, scaled, work - col * scaled)
    return work[:, K:]


def kernel(
    schur_hbm, precond_hbm, rs_ref, match_ref, x_out, r_out,
    a_mat, m_mat, rperm, msrc, rp, lz, mnext, u, full, hold, vsrc, perm_src, cont, vz,
    ar_src, ar_x, ar_y, ar_z, parts,
    mat_sem, init_sem, near_sem, gat_sem, ar_sem, send_sem,
):
    sx, sy = lax.axis_index("sx"), lax.axis_index("sy")
    nsx = NY * NZL
    y, zl = sx // NZL, sx % NZL
    zh, xc = sy // NXC, sy % NXC
    oz = 1 - zh
    z = zh * NZL + zl
    left, right = (sx + nsx - 1) % nsx, (sx + 1) % nsx
    far = oz * NXC + xc

    def x_peer(d):
        return (sx, zh * NXC + (xc + d) % NXC)

    def y_peer(d):
        return (((y + d) % NY) * NZL + zl, sy)

    def z_peer(d):
        other = (z + d) % NZ
        return (y * NZL + other % NZL, (other // NZL) * NXC + xc)

    peers = (
        [x_peer(d) for d in range(1, NXC)] + [y_peer(d) for d in range(1, NY)] + [z_peer(d) for d in range(1, NZ)]
        + [(left, sy), (right, sy), (left, far), (right, far)]
    )
    barrier = pltpu.get_barrier_semaphore()
    for peer in peers:
        pl.semaphore_signal(barrier, inc=1, device_id=peer, device_id_type=MESH)
    load_m = pltpu.make_async_copy(precond_hbm, m_mat, mat_sem.at[0])
    load_a = pltpu.make_async_copy(schur_hbm, a_mat, mat_sem.at[1])
    load_m.start()
    load_a.start()

    def copy(src, dst, recv, peer):
        return pltpu.make_async_remote_copy(
            src_ref=src, dst_ref=dst, send_sem=send_sem, recv_sem=recv, device_id=peer, device_id_type=MESH
        )

    sent = []

    def send(src, dst, recv, peer):
        copy(src, dst, recv, peer).start()
        sent.append(src)

    def arrived(ref, recv):
        copy(ref, ref, recv, (sx, sy)).wait_recv()

    spots = lax.broadcasted_iota(jnp.int32, (FB, FB), 0)
    mine = (spots == match_ref[...]).astype(BF16)
    rperm[...] = moved(rs_ref[...], mine, 0)
    msrc[...] = jnp.broadcast_to(match_ref[...], msrc.shape)
    pl.semaphore_wait(barrier, len(peers))

    send(rperm, rp.at[zh], init_sem.at[0], (left, sy))
    send(rperm, rp.at[zh], init_sem.at[0], (left, far))
    send(rs_ref, lz, init_sem.at[1], (sx, far))
    send(msrc, mnext, init_sem.at[2], (left, sy))

    def gather(slabs, recv):
        for d in range(1, NXC):
            send(slabs.at[xc], slabs.at[xc], recv, x_peer(d))

    def gathered(slabs, recv):
        arrived(slabs.at[pl.ds(0, NXC - 1)], recv)

    arrived(rp, init_sem.at[0])
    arrived(lz, init_sem.at[1])
    own = jnp.concatenate([rs_ref[...], rp[zh]], axis=1)
    other = jnp.concatenate([lz[...], rp[oz]], axis=1)

    def spread(no, slot, own, other, rounded):
        if rounded is not None:
            u[rounded, xc, zh] = own.astype(BF16)
            u[rounded, xc, oz] = other.astype(BF16)
            gather(u.at[rounded], gat_sem.at[4 + rounded])
        full[no, xc, zh] = own
        full[no, xc, oz] = other
        gather(full.at[no], gat_sem.at[no])

    spread(0, xc, own, other, 0)
    arrived(mnext, init_sem.at[2])
    following = (spots == mnext[0:1, :]).astype(BF16)

    def product(matrix, vector):
        total = jnp.zeros((K, 2 * FB), F32)
        for b in range(NXC * NZH):
            total += lax.dot_general(
                vector[b % NXC, b // NXC], matrix[:, 2 * FB * b : 2 * FB * (b + 1)],
                (((1,), (1,)), ((), ())), preferred_element_type=F32,
            )
        return total

    def tell(no, value):
        vsrc[no] = value
        send(vsrc.at[no], vz.at[no], near_sem.at[no, 0], (sx, far))
        perm_src[no, 0] = moved(value[:, FB:], following, 1)
        send(perm_src.at[no, 0], cont.at[no, zh, 0], near_sem.at[no, 1], (right, sy))
        send(perm_src.at[no, 0], cont.at[no, zh, 0], near_sem.at[no, 1], (right, far))
        perm_src[no, 1] = moved(value[:, :FB], mine, 0)
        send(perm_src.at[no, 1], cont.at[no, zh, 1], near_sem.at[no, 1], (left, sy))
        send(perm_src.at[no, 1], cont.at[no, zh, 1], near_sem.at[no, 1], (left, far))

    def assembled(no):
        arrived(vz.at[no], near_sem.at[no, 0])
        arrived(cont.at[no], near_sem.at[no, 1])
        own = vsrc[no] + jnp.concatenate([cont[no, zh, 0], cont[no, zh, 1]], axis=1)
        other = vz[no] + jnp.concatenate([cont[no, oz, 0], cont[no, oz, 1]], axis=1)
        return own, other

    def phase(no, step, value, slots, peer, me, n):
        slots[no, me] = value
        for d in range(1, n):
            send(slots.at[no, me], slots.at[no, me], ar_sem.at[no, step], peer(d))

    def phase_end(no, step, slots, n):
        arrived(slots.at[no, pl.ds(0, n - 1)], ar_sem.at[no, step])
        total = slots[no, 0]
        for i in range(1, n):
            total = total + slots[no, i]
        return total

    def reduce_x(no, value):
        phase(no, 0, value, ar_x, x_peer, xc, NXC)

    def reduce_y(no):
        phase(no, 1, phase_end(no, 0, ar_x, NXC), ar_y, y_peer, y, NY)

    def reduce_z(no):
        phase(no, 2, phase_end(no, 1, ar_y, NY), ar_z, z_peer, z, NZ)

    def reduced(no):
        return phase_end(no, 2, ar_z, NZ)

    def split_full(no):
        def body(i, carry):
            for j in range(NZH):
                for p, piece in enumerate(split3(full[no, i, j])):
                    parts[i, j, p] = piece
            return carry

        lax.fori_loop(0, NXC, body, 0)

    def stacked(i, j):
        return value_stack(parts[i, j, 0], parts[i, j, 1], parts[i, j, 2])

    load_m.wait()
    gathered(u.at[0], gat_sem.at[4])
    value = product(m_mat, u.at[0])
    tell(0, value)
    gamma_part = gram_part(own, value)
    own, other = assembled(0)
    spread(1, xc, own, other, 1)

    load_a.wait()
    gathered(u.at[1], gat_sem.at[5])
    value = product(a_mat, u.at[1])
    delta_part = gram_part(own, value)
    reduce_x(0, jnp.concatenate([gamma_part, delta_part], axis=0))
    tell(1, value)
    reduce_y(0)
    own, other = assembled(1)
    spread(2, xc, own, other, None)
    reduce_z(0)
    gathered(full.at[0], gat_sem.at[0])
    gathered(full.at[1], gat_sem.at[1])
    gathered(full.at[2], gat_sem.at[2])
    split_full(2)
    grams = reduced(0)
    gamma = unpacked(grams[:8])
    alpha = coeff_stack(solve(unpacked(grams[8:]), gamma))

    def residual_block(i, carry):
        for j in range(NZH):
            new = full[0, i, j] - combine(alpha, stacked(i, j))
            hold[0, i, j] = new
            u[2, i, j] = new.astype(BF16)
        return carry

    lax.fori_loop(0, NXC, residual_block, 0)

    value = product(m_mat, u.at[2])
    own_r = hold[0, xc, zh]
    blank = jnp.zeros((8, FB), F32)
    reduce_x(1, jnp.concatenate([gram_part(own_r, value), blank], axis=0))
    tell(2, value)
    reduce_y(1)
    own, other = assembled(2)
    spread(3, xc, own, other, None)
    reduce_z(1)
    eye = (lax.broadcasted_iota(jnp.int32, (K, K), 0) == lax.broadcasted_iota(jnp.int32, (K, K), 1)).astype(F32)
    ginv = coeff_stack(solve(gamma, eye))
    first_x = combine(alpha, value_stack(*split3(full[1, xc, zh][:, :FB])))
    split_full(1)

    def scaled_block(i, carry):
        for j in range(NZH):
            scaled = combine(ginv, stacked(i, j))
            for p, piece in enumerate(split3(scaled)):
                parts[i, j, p] = piece
        return carry

    lax.fori_loop(0, NXC, scaled_block, 0)
    gathered(full.at[3], gat_sem.at[3])
    gnew = unpacked(reduced(1)[:8])
    gnews = coeff_stack(gnew)

    def search_block(i, carry):
        for j in range(NZH):
            new = full[3, i, j] + combine(gnews, stacked(i, j))
            hold[1, i, j] = new
            u[3, i, j] = new.astype(BF16)
        return carry

    lax.fori_loop(0, NXC, search_block, 0)

    value = product(a_mat, u.at[3])
    own_p = hold[1, xc, zh]
    reduce_x(2, jnp.concatenate([gram_part(own_p, value), blank], axis=0))
    perm_src[3, 0] = moved(value[:, FB:], following, 1)
    send(perm_src.at[3, 0], cont.at[3, 0, 0], near_sem.at[3, 1], (right, sy))
    reduce_y(2)
    reduce_z(2)
    arrived(cont.at[3, 0, 0], near_sem.at[3, 1])
    q_stack = value_stack(*split3(value[:, :FB] + cont[3, 0, 0]))
    p_stack = value_stack(*split3(own_p[:, :FB]))
    alpha = coeff_stack(solve(unpacked(reduced(2)[:8]), gnew))
    x_out[...] = first_x + combine(alpha, p_stack)
    r_out[...] = own_r[:, :FB] - combine(alpha, q_stack)
    for src in sent:
        copy(src, src, init_sem.at[0], (sx, sy)).wait_send()


def shards(schur, precond, right_side, matching):
    block = jax.ShapeDtypeStruct((K, FB), F32)
    any_space = pl.BlockSpec(memory_space=pl.ANY)
    vmem = pl.BlockSpec(memory_space=pltpu.VMEM)
    rows, cols = schur.shape[1:]
    wide = 2 * FB
    x, r = pl.pallas_call(
        kernel,
        out_shape=(block, block),
        in_specs=[any_space, any_space, vmem, vmem],
        out_specs=(vmem, vmem),
        scratch_shapes=[
            pltpu.VMEM((rows, cols), BF16), pltpu.VMEM((rows, cols), BF16),
            pltpu.VMEM((K, FB), F32), pltpu.VMEM((8, FB), jnp.int32),
            pltpu.VMEM((NZH, K, FB), F32), pltpu.VMEM((K, FB), F32), pltpu.VMEM((8, FB), jnp.int32),
            pltpu.VMEM((4, NXC, NZH, K, wide), BF16),
            pltpu.VMEM((4, NXC, NZH, K, wide), F32), pltpu.VMEM((2, NXC, NZH, K, wide), F32),
            pltpu.VMEM((3, K, wide), F32), pltpu.VMEM((4, 2, K, FB), F32),
            pltpu.VMEM((4, NZH, 2, K, FB), F32), pltpu.VMEM((3, K, wide), F32),
            pltpu.VMEM((8, FB), F32),
            pltpu.VMEM((3, NXC, 16, FB), F32), pltpu.VMEM((3, NY, 16, FB), F32), pltpu.VMEM((3, NZ, 16, FB), F32),
            pltpu.VMEM((NXC, NZH, 3, K, wide), BF16),
            pltpu.SemaphoreType.DMA((2,)), pltpu.SemaphoreType.DMA((3,)), pltpu.SemaphoreType.DMA((4, 2)),
            pltpu.SemaphoreType.DMA((6,)), pltpu.SemaphoreType.DMA((3, 3)), pltpu.SemaphoreType.DMA,
        ],
        compiler_params=pltpu.CompilerParams(collective_id=0, has_side_effects=True, vmem_limit_bytes=40 * 2**20),
        name="schwarz_cg",
    )(schur[0], precond[0], right_side[0], matching)
    return x[None], r[None]


def solution(mesh):
    in_specs = (P("sx", "sy", None), P("sx", "sy", None), P("sx", None, "sy"), P("sx", "sy"))
    out_specs = (P("sx", None, "sy"), P("sx", None, "sy"))
    return jax.shard_map(shards, mesh=mesh, in_specs=in_specs, out_specs=out_specs, check_vma=False)
```

time: 575 us -> 121 us (0.21)
  blocking collectives: 458 us -> 0 us
  Pallas kernels: 0 us -> 115 us
  waiting for transfers between devices: 38 us -> 0 us
  starting transfers between devices: 33.9 us -> 0 us
  other arithmetic: 25.6 us -> 0 us
  matrix products: 10.1 us -> 0 us
    psum x3 -> x0, blocking collectives: 314 us -> none  [gram(): total = lax.psum(partial_sum, ('sx', 'sy'))]
    all_gather x4 -> x0, blocking collectives: 144 us -> none  [apply_op(): lax.all_gather(local, 'sy', axis=1, tiled=True)]
    pallas_call x0 -> x1, Pallas kernels: none -> 115 us  [shards(): pl.pallas_call(kernel, out_shape=(block, block), in_specs=[any_space, any...]
    ppermute x8 -> x0, waiting for transfers between devices: 38 us -> none  [passed_along(): return lax.ppermute(block, axis, route)]
    ppermute x8 -> x0, starting transfers between devices: 33.9 us -> none  [passed_along(): return lax.ppermute(block, axis, route)]
    another operation x15 -> x0, other arithmetic: 20 us -> none  [the longest x9 10.8 us: solve_spd(): lower = jnp.linalg.cholesky(matrix)]
    dot_general x13 -> x0, matrix products: 9.05 us -> none  [the longest x4 6.07 us: apply_op(): lax.dot_general(lax.all_gather(local, 'sy', axis=1, tiled=True), matrix,...]
    gather x16 -> x0, local copies, waits for them, and re-layouts: 5.95 us -> none  [the longest x8 3.14 us: apply_op(): sent = jnp.take(block, match_loc, axis=1)]
  transfers between devices with their start and end apart: 8 -> 0, of which waited for: 7 -> 0; matrix products, arithmetic and copies ran while one was open for 1% -> 0% of each run, Pallas kernels for 0% -> 0%
where the time goes in v1:
time: 121 us
  Pallas kernels  115 us (95%)
  local copies, waits for them, and re-layouts  5.76 us (5%)
    pallas_call x1, Pallas kernels, shards(): pl.pallas_call(kernel, out_shape=(block, block), in_specs=[any_space, any...  115 us
    unnamed x10, local copies, waits for them, and re-layouts  5.76 us

profile of v1, /device:TPU:1, one launch (start us, length us, event | category | flops | bytes accessed | tf_op | source)
XLA Modules:
  0.0 121.0 jit_solution(6422559488793909249)
XLA Ops:
  0.6 0.0 copy-start
  0.6 1.6 %copy-done = bf16[1,256,4096]{2,1,0:T(8,128)(2,1)S(1)} copy-done((bf16[1,256,4096]{2,1,0:T(8,128)(2,1)S(1)}, bf16[1,256,4096]{2,1,0:T(8,128)(2,1)}, u32[]{:S(2)}) %copy-start) | copy-done | bytes 2097176
  2.2 0.0 copy-start.1
  2.2 1.6 %copy-done.1 = bf16[1,256,4096]{2,1,0:T(8,128)(2,1)S(1)} copy-done((bf16[1,256,4096]{2,1,0:T(8,128)(2,1)S(1)}, bf16[1,256,4096]{2,1,0:T(8,128)(2,1)}, u32[]{:S(2)}) %copy-start.1) | copy-done | bytes 2097176
  3.8 0.0 copy-start.2
  3.8 0.7 copy-done.2
  4.5 0.0 copy-start.3
  4.5 0.7 copy-done.3
  5.2 114.6 %schwarz_cg.1 = (f32[32,128]{1,0:T(8,128)S(1)}, f32[32,128]{1,0:T(8,128)S(1)}) custom-call(bf16[256,4096]{1,0:T(8,128)(2,1)S(1)} %bitcast.5, bf16[256,4096]{1,0:T(8,128)(2,1)S(1)} %bitcast.6, f32[32,128]{1,0:T(8,128)S(1)} %bitcast.7, s32[1,128]{1,0:T(1,128)S(1)} %copy-done.3), custom_call_target="tpu_custom_call" | custom-call | tf_op jit(solution)/shard_map/schwarz_cg/pallas_call | solution.py:310
  119.8 0.6 copy.8
  120.4 0.6 copy.9
Async XLA Ops:
  0.6 1.6 %copy-start = (bf16[1,256,4096]{2,1,0:T(8,128)(2,1)S(1)}, bf16[1,256,4096]{2,1,0:T(8,128)(2,1)}, u32[]{:S(2)}) copy-start(bf16[1,256,4096]{2,1,0:T(8,128)(2,1)} %param.4) | copy-start | bytes 6291460
  2.2 1.6 %copy-start.1 = (bf16[1,256,4096]{2,1,0:T(8,128)(2,1)S(1)}, bf16[1,256,4096]{2,1,0:T(8,128)(2,1)}, u32[]{:S(2)}) copy-start(bf16[1,256,4096]{2,1,0:T(8,128)(2,1)} %param.5) | copy-start | bytes 6291460
  3.8 0.7 copy-start.2
  4.5 0.7 copy-start.3

commit v2 on v1

--- a/solution.py
+++ b/solution.py
@@ -54,21 +54,29 @@
     return jnp.concatenate([packed[:, K * a : K * a + K] for a in range(4)], axis=0)
 
 
+PANEL = 8
+
+
 def solve(matrix, rhs):
     work = jnp.concatenate([matrix, rhs], axis=1)
     row_no = lax.broadcasted_iota(jnp.int32, work.shape, 0)
-    for k in range(K):
-        col = work[:, k : k + 1]
-        row = work[k : k + 1, :]
-        scaled = row * (1.0 / work[k : k + 1, k : k + 1])
-        work = jnp.where(row_no == k, scaled, work - col * scaled)
+    for first in range(0, K, PANEL):
+        cols = [jnp.broadcast_to(work[:, k : k + 1], work.shape) for k in range(first, first + PANEL)]
+        for q in range(PANEL):
+            k = first + q
+            inverse = 1.0 / cols[q][k : k + 1]
+            row = work[k : k + 1] * inverse
+            work = jnp.where(row_no == k, row, work - cols[q] * row)
+            for p in range(q + 1, PANEL):
+                factor = cols[p][k : k + 1] * inverse
+                cols[p] = jnp.where(row_no == k, factor, cols[p] - cols[q] * factor)
     return work[:, K:]
 
 
 def kernel(
-    schur_hbm, precond_hbm, rs_ref, match_ref, x_out, r_out,
-    a_mat, m_mat, rperm, msrc, rp, lz, mnext, u, full, hold, vsrc, perm_src, cont, vz,
-    ar_src, ar_x, ar_y, ar_z, parts,
+    schur_hbm, precond_hbm, rs_hbm, match_hbm, x_out, r_out,
+    rs_ref, match_ref, a_rows, m_rows, a_mat, m_mat, rperm, msrc, rp, lz, mnext, u, full, hold, vsrc, perm_src, cont, vz,
+    ar_x, ar_y, ar_z, parts,
     mat_sem, init_sem, near_sem, gat_sem, ar_sem, send_sem,
 ):
     sx, sy = lax.axis_index("sx"), lax.axis_index("sy")
@@ -97,8 +105,12 @@
     barrier = pltpu.get_barrier_semaphore()
     for peer in peers:
         pl.semaphore_signal(barrier, inc=1, device_id=peer, device_id_type=MESH)
-    load_m = pltpu.make_async_copy(precond_hbm, m_mat, mat_sem.at[0])
-    load_a = pltpu.make_async_copy(schur_hbm, a_mat, mat_sem.at[1])
+    load_m = pltpu.make_async_copy(precond_hbm, m_rows, mat_sem.at[0])
+    load_a = pltpu.make_async_copy(schur_hbm, a_rows, mat_sem.at[1])
+    load_r = pltpu.make_async_copy(rs_hbm, rs_ref, mat_sem.at[2])
+    load_p = pltpu.make_async_copy(match_hbm, match_ref, mat_sem.at[3])
+    load_r.start()
+    load_p.start()
     load_m.start()
     load_a.start()
 
@@ -116,6 +128,8 @@
     def arrived(ref, recv):
         copy(ref, ref, recv, (sx, sy)).wait_recv()
 
+    load_p.wait()
+    load_r.wait()
     spots = lax.broadcasted_iota(jnp.int32, (FB, FB), 0)
     mine = (spots == match_ref[...]).astype(BF16)
     rperm[...] = moved(rs_ref[...], mine, 0)
@@ -127,6 +141,15 @@
     send(rs_ref, lz, init_sem.at[1], (sx, far))
     send(msrc, mnext, init_sem.at[2], (left, sy))
 
+    def transposed(source, target):
+        for b in range(NXC * NZH):
+            target[2 * FB * b : 2 * FB * (b + 1), :] = source[:, 2 * FB * b : 2 * FB * (b + 1)].T
+
+    load_m.wait()
+    transposed(m_rows, m_mat)
+    load_a.wait()
+    transposed(a_rows, a_mat)
+
     def gather(slabs, recv):
         for d in range(1, NXC):
             send(slabs.at[xc], slabs.at[xc], recv, x_peer(d))
@@ -139,7 +162,7 @@
     own = jnp.concatenate([rs_ref[...], rp[zh]], axis=1)
     other = jnp.concatenate([lz[...], rp[oz]], axis=1)
 
-    def spread(no, slot, own, other, rounded):
+    def spread(no, own, other, rounded):
         if rounded is not None:
             u[rounded, xc, zh] = own.astype(BF16)
             u[rounded, xc, oz] = other.astype(BF16)
@@ -148,7 +171,7 @@
         full[no, xc, oz] = other
         gather(full.at[no], gat_sem.at[no])
 
-    spread(0, xc, own, other, 0)
+    spread(0, own, other, 0)
     arrived(mnext, init_sem.at[2])
     following = (spots == mnext[0:1, :]).astype(BF16)
 
@@ -156,14 +179,16 @@
         total = jnp.zeros((K, 2 * FB), F32)
         for b in range(NXC * NZH):
             total += lax.dot_general(
-                vector[b % NXC, b // NXC], matrix[:, 2 * FB * b : 2 * FB * (b + 1)],
-                (((1,), (1,)), ((), ())), preferred_element_type=F32,
+                vector[b % NXC, b // NXC], matrix[2 * FB * b : 2 * FB * (b + 1), :],
+                (((1,), (0,)), ((), ())), preferred_element_type=F32,
             )
         return total
 
-    def tell(no, value):
+    def tell_partner(no, value):
         vsrc[no] = value
         send(vsrc.at[no], vz.at[no], near_sem.at[no, 0], (sx, far))
+
+    def tell(no, value):
         perm_src[no, 0] = moved(value[:, FB:], following, 1)
         send(perm_src.at[no, 0], cont.at[no, zh, 0], near_sem.at[no, 1], (right, sy))
         send(perm_src.at[no, 0], cont.at[no, zh, 0], near_sem.at[no, 1], (right, far))
@@ -209,36 +234,37 @@
                     parts[i, j, p] = piece
             return carry
 
-        lax.fori_loop(0, NXC, body, 0)
+        for i in range(NXC):
+            body(i, 0)
 
     def stacked(i, j):
         return value_stack(parts[i, j, 0], parts[i, j, 1], parts[i, j, 2])
 
-    load_m.wait()
     gathered(u.at[0], gat_sem.at[4])
     value = product(m_mat, u.at[0])
+    tell_partner(0, value)
     tell(0, value)
-    gamma_part = gram_part(own, value)
+    reduce_x(0, gram_part(own, value))
     own, other = assembled(0)
-    spread(1, xc, own, other, 1)
-
-    load_a.wait()
+    spread(1, own, other, 1)
+    reduce_y(0)
+
     gathered(u.at[1], gat_sem.at[5])
     value = product(a_mat, u.at[1])
-    delta_part = gram_part(own, value)
-    reduce_x(0, jnp.concatenate([gamma_part, delta_part], axis=0))
+    tell_partner(1, value)
+    reduce_x(1, gram_part(own, value))
     tell(1, value)
-    reduce_y(0)
+    reduce_z(0)
+    reduce_y(1)
     own, other = assembled(1)
-    spread(2, xc, own, other, None)
-    reduce_z(0)
+    spread(2, own, other, None)
+    reduce_z(1)
     gathered(full.at[0], gat_sem.at[0])
     gathered(full.at[1], gat_sem.at[1])
     gathered(full.at[2], gat_sem.at[2])
     split_full(2)
-    grams = reduced(0)
-    gamma = unpacked(grams[:8])
-    alpha = coeff_stack(solve(unpacked(grams[8:]), gamma))
+    gamma = unpacked(reduced(0))
+    alpha = coeff_stack(solve(unpacked(reduced(1)), gamma))
 
     def residual_block(i, carry):
         for j in range(NZH):
@@ -247,17 +273,18 @@
             u[2, i, j] = new.astype(BF16)
         return carry
 
-    lax.fori_loop(0, NXC, residual_block, 0)
+    for i in range(NXC):
+        residual_block(i, 0)
 
     value = product(m_mat, u.at[2])
     own_r = hold[0, xc, zh]
-    blank = jnp.zeros((8, FB), F32)
-    reduce_x(1, jnp.concatenate([gram_part(own_r, value), blank], axis=0))
+    tell_partner(2, value)
+    reduce_x(2, gram_part(own_r, value))
     tell(2, value)
-    reduce_y(1)
+    reduce_y(2)
     own, other = assembled(2)
-    spread(3, xc, own, other, None)
-    reduce_z(1)
+    spread(3, own, other, None)
+    reduce_z(2)
     eye = (lax.broadcasted_iota(jnp.int32, (K, K), 0) == lax.broadcasted_iota(jnp.int32, (K, K), 1)).astype(F32)
     ginv = coeff_stack(solve(gamma, eye))
     first_x = combine(alpha, value_stack(*split3(full[1, xc, zh][:, :FB])))
@@ -270,9 +297,10 @@
                 parts[i, j, p] = piece
         return carry
 
-    lax.fori_loop(0, NXC, scaled_block, 0)
+    for i in range(NXC):
+        scaled_block(i, 0)
     gathered(full.at[3], gat_sem.at[3])
-    gnew = unpacked(reduced(1)[:8])
+    gnew = unpacked(reduced(2))
     gnews = coeff_stack(gnew)
 
     def search_block(i, carry):
@@ -282,19 +310,20 @@
             u[3, i, j] = new.astype(BF16)
         return carry
 
-    lax.fori_loop(0, NXC, search_block, 0)
+    for i in range(NXC):
+        search_block(i, 0)
 
     value = product(a_mat, u.at[3])
     own_p = hold[1, xc, zh]
-    reduce_x(2, jnp.concatenate([gram_part(own_p, value), blank], axis=0))
+    reduce_x(3, gram_part(own_p, value))
     perm_src[3, 0] = moved(value[:, FB:], following, 1)
     send(perm_src.at[3, 0], cont.at[3, 0, 0], near_sem.at[3, 1], (right, sy))
-    reduce_y(2)
-    reduce_z(2)
+    reduce_y(3)
+    reduce_z(3)
     arrived(cont.at[3, 0, 0], near_sem.at[3, 1])
     q_stack = value_stack(*split3(value[:, :FB] + cont[3, 0, 0]))
     p_stack = value_stack(*split3(own_p[:, :FB]))
-    alpha = coeff_stack(solve(unpacked(reduced(2)[:8]), gnew))
+    alpha = coeff_stack(solve(unpacked(reduced(3)), gnew))
     x_out[...] = first_x + combine(alpha, p_stack)
     r_out[...] = own_r[:, :FB] - combine(alpha, q_stack)
     for src in sent:
@@ -303,30 +332,31 @@
 
 def shards(schur, precond, right_side, matching):
     block = jax.ShapeDtypeStruct((K, FB), F32)
-    any_space = pl.BlockSpec(memory_space=pl.ANY)
+    hbm = pl.BlockSpec(memory_space=pltpu.HBM)
     vmem = pl.BlockSpec(memory_space=pltpu.VMEM)
     rows, cols = schur.shape[1:]
     wide = 2 * FB
     x, r = pl.pallas_call(
         kernel,
         out_shape=(block, block),
-        in_specs=[any_space, any_space, vmem, vmem],
+        in_specs=[hbm, hbm, hbm, hbm],
         out_specs=(vmem, vmem),
         scratch_shapes=[
+            pltpu.VMEM((K, FB), F32), pltpu.VMEM((1, FB), jnp.int32),
             pltpu.VMEM((rows, cols), BF16), pltpu.VMEM((rows, cols), BF16),
+            pltpu.VMEM((cols, rows), BF16), pltpu.VMEM((cols, rows), BF16),
             pltpu.VMEM((K, FB), F32), pltpu.VMEM((8, FB), jnp.int32),
             pltpu.VMEM((NZH, K, FB), F32), pltpu.VMEM((K, FB), F32), pltpu.VMEM((8, FB), jnp.int32),
             pltpu.VMEM((4, NXC, NZH, K, wide), BF16),
             pltpu.VMEM((4, NXC, NZH, K, wide), F32), pltpu.VMEM((2, NXC, NZH, K, wide), F32),
             pltpu.VMEM((3, K, wide), F32), pltpu.VMEM((4, 2, K, FB), F32),
             pltpu.VMEM((4, NZH, 2, K, FB), F32), pltpu.VMEM((3, K, wide), F32),
-            pltpu.VMEM((8, FB), F32),
-            pltpu.VMEM((3, NXC, 16, FB), F32), pltpu.VMEM((3, NY, 16, FB), F32), pltpu.VMEM((3, NZ, 16, FB), F32),
+            pltpu.VMEM((4, NXC, 8, FB), F32), pltpu.VMEM((4, NY, 8, FB), F32), pltpu.VMEM((4, NZ, 8, FB), F32),
             pltpu.VMEM((NXC, NZH, 3, K, wide), BF16),
-            pltpu.SemaphoreType.DMA((2,)), pltpu.SemaphoreType.DMA((3,)), pltpu.SemaphoreType.DMA((4, 2)),
-            pltpu.SemaphoreType.DMA((6,)), pltpu.SemaphoreType.DMA((3, 3)), pltpu.SemaphoreType.DMA,
+            pltpu.SemaphoreType.DMA((4,)), pltpu.SemaphoreType.DMA((3,)), pltpu.SemaphoreType.DMA((4, 2)),
+            pltpu.SemaphoreType.DMA((6,)), pltpu.SemaphoreType.DMA((4, 3)), pltpu.SemaphoreType.DMA,
         ],
-        compiler_params=pltpu.CompilerParams(collective_id=0, has_side_effects=True, vmem_limit_bytes=40 * 2**20),
+        compiler_params=pltpu.CompilerParams(collective_id=0, has_side_effects=True, vmem_limit_bytes=64 * 2**20),
         name="schwarz_cg",
     )(schur[0], precond[0], right_side[0], matching)
     return x[None], r[None]

time: 121 us -> 104 us (0.86)
  Pallas kernels: 115 us -> 100 us
  local copies, waits for them, and re-layouts: 5.76 us -> 2.65 us
    pallas_call x1, Pallas kernels: 115 us -> 100 us  [shards(): pl.pallas_call(kernel, out_shape=(block, block), in_specs=[hbm, hbm, hbm,...]
    unnamed x10 -> x2, local copies, waits for them, and re-layouts: 5.76 us -> 2.65 us
where the time goes in v2:
time: 104 us; the launch traced here: 103 us
  Pallas kernels  100 us (96%)
  local copies, waits for them, and re-layouts  2.65 us (3%)
    pallas_call x1, Pallas kernels, shards(): pl.pallas_call(kernel, out_shape=(block, block), in_specs=[hbm, hbm, hbm,...  100 us
    unnamed x2, local copies, waits for them, and re-layouts  2.65 us

profile of v2, /device:TPU:1, one launch (start us, length us, event | category | flops | bytes accessed | tf_op | source)
XLA Modules:
  0.0 103.3 jit_solution(2657828041069401219)
XLA Ops:
  0.6 100.0 %schwarz_cg.1 = (f32[32,128]{1,0:T(8,128)}, f32[32,128]{1,0:T(8,128)}) custom-call(bf16[256,4096]{1,0:T(8,128)(2,1)} %bitcast.5, bf16[256,4096]{1,0:T(8,128)(2,1)} %bitcast.6, f32[32,128]{1,0:T(8,128)} %bitcast.7, s32[1,128]{1,0:T(1,128)} %match_hbm.1), custom_call_target="tpu_custom_call" | custom-call | tf_op jit(solution)/shard_map/schwarz_cg/pallas_call | solution.py:339
  100.7 1.3 %copy.8 = f32[1,32,128]{2,1,0:T(8,128)} copy(f32[1,32,128]{2,1,0:T(8,128)} %bitcast.9) | data formatting | bytes 32768
  102.0 1.3 %copy.9 = f32[1,32,128]{2,1,0:T(8,128)} copy(f32[1,32,128]{2,1,0:T(8,128)} %bitcast.8) | data formatting | bytes 32768

commit v3 on v2

--- a/solution.py
+++ b/solution.py
@@ -12,6 +12,10 @@
 NY, NZL, NZH, NXC = 8, 6, 2, 8
 NZ = NZL * NZH
 K, FB = 32, 128
+
+
+def far_first(n):
+    return sorted(range(1, n), key=lambda d: -min(d, n - d))
 
 
 def split3(value):
@@ -74,7 +78,7 @@
 
 
 def kernel(
-    schur_hbm, precond_hbm, rs_hbm, match_hbm, x_out, r_out,
+    schur_hbm, precond_hbm, rs_hbm, match_hbm, out,
     rs_ref, match_ref, a_rows, m_rows, a_mat, m_mat, rperm, msrc, rp, lz, mnext, u, full, hold, vsrc, perm_src, cont, vz,
     ar_x, ar_y, ar_z, parts,
     mat_sem, init_sem, near_sem, gat_sem, ar_sem, send_sem,
@@ -151,7 +155,7 @@
     transposed(a_rows, a_mat)
 
     def gather(slabs, recv):
-        for d in range(1, NXC):
+        for d in far_first(NXC):
             send(slabs.at[xc], slabs.at[xc], recv, x_peer(d))
 
     def gathered(slabs, recv):
@@ -169,7 +173,8 @@
             gather(u.at[rounded], gat_sem.at[4 + rounded])
         full[no, xc, zh] = own
         full[no, xc, oz] = other
-        gather(full.at[no], gat_sem.at[no])
+        if rounded is None:
+            gather(full.at[no], gat_sem.at[no])
 
     spread(0, own, other, 0)
     arrived(mnext, init_sem.at[2])
@@ -205,7 +210,7 @@
 
     def phase(no, step, value, slots, peer, me, n):
         slots[no, me] = value
-        for d in range(1, n):
+        for d in far_first(n):
             send(slots.at[no, me], slots.at[no, me], ar_sem.at[no, step], peer(d))
 
     def phase_end(no, step, slots, n):
@@ -241,6 +246,7 @@
         return value_stack(parts[i, j, 0], parts[i, j, 1], parts[i, j, 2])
 
     gathered(u.at[0], gat_sem.at[4])
+    gather(full.at[0], gat_sem.at[0])
     value = product(m_mat, u.at[0])
     tell_partner(0, value)
     tell(0, value)
@@ -260,8 +266,8 @@
     spread(2, own, other, None)
     reduce_z(1)
     gathered(full.at[0], gat_sem.at[0])
-    gathered(full.at[1], gat_sem.at[1])
     gathered(full.at[2], gat_sem.at[2])
+    gather(full.at[1], gat_sem.at[1])
     split_full(2)
     gamma = unpacked(reduced(0))
     alpha = coeff_stack(solve(unpacked(reduced(1)), gamma))
@@ -288,6 +294,7 @@
     eye = (lax.broadcasted_iota(jnp.int32, (K, K), 0) == lax.broadcasted_iota(jnp.int32, (K, K), 1)).astype(F32)
     ginv = coeff_stack(solve(gamma, eye))
     first_x = combine(alpha, value_stack(*split3(full[1, xc, zh][:, :FB])))
+    gathered(full.at[1], gat_sem.at[1])
     split_full(1)
 
     def scaled_block(i, carry):
@@ -324,23 +331,22 @@
     q_stack = value_stack(*split3(value[:, :FB] + cont[3, 0, 0]))
     p_stack = value_stack(*split3(own_p[:, :FB]))
     alpha = coeff_stack(solve(unpacked(reduced(3)), gnew))
-    x_out[...] = first_x + combine(alpha, p_stack)
-    r_out[...] = own_r[:, :FB] - combine(alpha, q_stack)
+    out[0] = first_x + combine(alpha, p_stack)
+    out[1] = own_r[:, :FB] - combine(alpha, q_stack)
     for src in sent:
         copy(src, src, init_sem.at[0], (sx, sy)).wait_send()
 
 
 def shards(schur, precond, right_side, matching):
-    block = jax.ShapeDtypeStruct((K, FB), F32)
     hbm = pl.BlockSpec(memory_space=pltpu.HBM)
     vmem = pl.BlockSpec(memory_space=pltpu.VMEM)
     rows, cols = schur.shape[1:]
     wide = 2 * FB
-    x, r = pl.pallas_call(
+    out = pl.pallas_call(
         kernel,
-        out_shape=(block, block),
+        out_shape=jax.ShapeDtypeStruct((2, K, FB), F32),
         in_specs=[hbm, hbm, hbm, hbm],
-        out_specs=(vmem, vmem),
+        out_specs=vmem,
         scratch_shapes=[
             pltpu.VMEM((K, FB), F32), pltpu.VMEM((1, FB), jnp.int32),
             pltpu.VMEM((rows, cols), BF16), pltpu.VMEM((rows, cols), BF16),
@@ -359,7 +365,7 @@
         compiler_params=pltpu.CompilerParams(collective_id=0, has_side_effects=True, vmem_limit_bytes=64 * 2**20),
         name="schwarz_cg",
     )(schur[0], precond[0], right_side[0], matching)
-    return x[None], r[None]
+    return out[0:1], out[1:2]
 
 
 def solution(mesh):

time: 104 us -> 98.4 us (0.946)
  Pallas kernels: 100 us -> 96.1 us
  local copies, waits for them, and re-layouts: 2.65 us -> 1.35 us
    pallas_call x1, Pallas kernels: 100 us -> 96.1 us  [shards(): pl.pallas_call(kernel, out_shape=jax.ShapeDtypeStruct((2, K, FB), F32), i...]
    unnamed x2 -> x0, local copies, waits for them, and re-layouts: 2.65 us -> none
    slice x0 -> x1, local copies, waits for them, and re-layouts: none -> 1.35 us  [shards(): return (out[0:1], out[1:2])]
where the time goes in v3:
time: 98.4 us; the launch traced here: 98.1 us
  Pallas kernels  96.1 us (98%)
  local copies, waits for them, and re-layouts  1.35 us (1%)
    pallas_call x1, Pallas kernels, shards(): pl.pallas_call(kernel, out_shape=jax.ShapeDtypeStruct((2, K, FB), F32), i...  96.1 us

profile of v3, /device:TPU:1, one launch (start us, length us, event | category | flops | bytes accessed | tf_op | source)
XLA Modules:
  0.0 98.1 jit_solution(2080220874097379694)
XLA Ops:
  0.6 96.1 %schwarz_cg.1 = f32[2,32,128]{2,1,0:T(8,128)} custom-call(bf16[256,4096]{1,0:T(8,128)(2,1)} %bitcast.3, bf16[256,4096]{1,0:T(8,128)(2,1)} %bitcast.4, f32[32,128]{1,0:T(8,128)} %bitcast.5, s32[1,128]{1,0:T(1,128)} %match_hbm.1), custom_call_target="tpu_custom_call" | custom-call | tf_op jit(solution)/shard_map/schwarz_cg/pallas_call | solution.py:345
  96.7 1.3 %fusion = (f32[1,32,128]{2,1,0:T(8,128)}, f32[1,32,128]{2,1,0:T(8,128)}) fusion(f32[2,32,128]{2,1,0:T(8,128)} %schwarz_cg.1), kind=kLoop, calls=%fused_computation | loop fusion | bytes 65536 | tf_op jit(solution)/shard_map/slice | solution.py:368
